TPU v7x, 128 devices: a whole 4x4x4 slice. The times are simulated.
128 devices in a mesh: replica: 8 (over z, x_lo), fsdp: 16 (over y, x_hi, core).
Axes of the slice: x: 4 (x_hi: 2, x_lo: 2; x = x_hi * 2 + x_lo), y: 4, z: 4, core: 2. Of those that a mesh axis runs over, the one named last changes fastest.
Arguments:
- codes: int32 [8, 3584, 7168], P('replica', None, 'fsdp'), may hold values from -8 to 7
- exponents: int32 [8, 28, 7168], P('replica', None, 'fsdp'), may hold values from -10 to -6
- params: float32 [3584, 7168], P('replica', 'fsdp'), may hold values from -0.09375 to 0.09375
- momentum: float32 [3584, 7168], P('replica', 'fsdp'), may hold values from -0.0625 to 0.0625
- attention: bfloat16 [8, 4096, 3584], P('replica', 'fsdp'), may hold values from -6 to 6
- residual: bfloat16 [8, 4096, 7168], P('replica', 'fsdp'), may hold values from -6 to 6
Outputs:
- params_out: float32 [3584, 7168], P('replica', 'fsdp')
- momentum_out: float32 [3584, 7168], P('replica', 'fsdp')
- hidden_out: bfloat16 [8, 4096, 7168], P('replica', 'fsdp')
All inputs are finite; a program needn't handle non-finite values.
Results may differ from a plain program's by a relative error of at most 0.0075.
Values may be sent and summed in bfloat16 or wider, within the bound.
A program may use at most 128 MiB of HBM per device.

v0:
```python
import jax
import jax.numpy as jnp
from jax import lax
from jax.sharding import PartitionSpec as P


def scale_of(exponents):
    scales = jnp.zeros(exponents.shape, jnp.float32)
    for exponent_value in range(-10, -5):
        scales = scales + jnp.where(
            exponents == exponent_value, jnp.float32(2.0**exponent_value), jnp.float32(0.0)
        )
    return scales


def dequantize(code_block, exponent_block):
    scales = scale_of(exponent_block)
    blocks = exponent_block.shape[0]
    width = code_block.shape[1]
    shaped = code_block.astype(jnp.float32).reshape(blocks, code_block.shape[0] // blocks, width)
    return (shaped * scales[:, None, :]).reshape(code_block.shape[0], width)


def shards(codes, exponents, params, momentum, attention, residual):
    delta_values = dequantize(codes[0], exponents[0])
    replicas = lax.axis_size("replica")
    share_rows = params.shape[0]
    summed = lax.psum(delta_values.astype(jnp.bfloat16), "replica").astype(jnp.float32)
    summed = lax.dynamic_slice_in_dim(summed, lax.axis_index("replica") * share_rows, share_rows, 0)
    outer_grad = summed / replicas
    momentum_out = 0.9 * momentum + outer_grad
    params_out = params - 0.7 * (outer_grad + 0.9 * momentum_out)
    out_block = params_out.astype(jnp.bfloat16)
    out_weight = lax.all_gather(out_block, "replica", axis=0, tiled=True)
    columns = jnp.dot(
        lax.all_gather(attention[0], "fsdp", axis=0, tiled=True),
        out_weight,
        preferred_element_type=jnp.float32,
    ).astype(jnp.bfloat16)
    rows_back = lax.all_to_all(columns, "fsdp", split_axis=0, concat_axis=1, tiled=True)
    hidden_out = (residual[0].astype(jnp.float32) + rows_back.astype(jnp.float32)).astype(
        jnp.bfloat16
    )
    return (params_out, momentum_out, hidden_out[None])


def solution(mesh):
    placed = (
        P("replica", None, "fsdp"),
        P("replica", None, "fsdp"),
        P("replica", "fsdp"),
        P("replica", "fsdp"),
        P("replica", "fsdp", None),
        P("replica", "fsdp", None),
    )
    return jax.shard_map(
        shards,
        mesh=mesh,
        in_specs=placed,
        out_specs=(P("replica", "fsdp"), P("replica", "fsdp"), P("replica", "fsdp", None)),
        check_vma=False,
    )
```

profile of v0, /device:TPU:1, one launch (start us, length us, event | category | flops | bytes accessed | tf_op | source)
XLA Modules:
  0.0 535.0 jit_solution(13549697594712806209)
XLA Ops:
  7.2 0.0 copy-start.3
  7.2 0.0 all-reduce.2.cloned.1.call-start
  7.2 8.0 %copy.11 = s32[1,3584,448]{2,1,0:T(8,128)} copy(s32[1,3584,448]{1,2,0:T(8,128)} %param.6) | data formatting | bytes 12845056 | tf_op args[0]
  15.2 0.0 copy-done.3
  15.3 0.2 fusion.10
  15.5 6.0 %fusion.3 = bf16[3584,448]{1,0:T(8,128)(2,1)} fusion(s32[1,3584,448]{2,1,0:T(8,128)} %copy.11, f32[28,448]{1,0:T(8,128)S(1)} %bitcast.30), kind=kLoop, calls=%fused_computation.5 | loop fusion | flops 4816896 | bytes 9683968 | tf_op jit(solution)/shard_map/convert_element_type | solution.py:28
  21.5 0.0 copy-start.1
  21.5 0.0 copy-start.2
  21.5 0.0 all-reduce.2.cloned.1.call-update
  21.5 0.0 all-gather.4.cloned.1.call-start
  21.6 166.6 %all-reduce.2.cloned.1.call-done = bf16[3584,448]{1,0:T(8,128)(2,1)} async-done(((bf16[3584,448]{1,0:T(8,128)(2,1)}), bf16[3584,448]{1,0:T(8,128)(2,1)}) %all-reduce.2.cloned.1.call-update) | async-done | bytes 3211280 | tf_op jit(solution)/shard_map/psum | solution.py:28
  188.1 0.0 copy-done.1
  188.1 0.0 copy-done.2
  188.1 2.7 fusion.11
  190.9 0.0 all-gather.4.cloned.1.call-update
  190.9 0.0 all-gather.6.cloned.1.call-start
  190.9 0.7 all-gather.6.cloned.1.call-update
  191.6 80.4 %all-gather.4.cloned.1.call-done = bf16[3584,448]{1,0:T(8,128)(2,1)} async-done(((bf16[448,448]{1,0:T(8,128)(2,1)}), bf16[3584,448]{1,0:T(8,128)(2,1)}) %all-gather.4.cloned.1.call-update) | async-done | bytes 3211280 | tf_op jit(solution)/shard_map/all_gather | solution.py:34
  272.0 169.5 %all-gather.6.cloned.1.call-done = bf16[1,4096,3584]{2,1,0:T(8,128)(2,1)} async-done(((bf16[1,256,3584]{2,1,0:T(8,128)(2,1)}), bf16[1,4096,3584]{2,1,0:T(8,128)(2,1)}) %all-gather.6.cloned.1.call-update) | async-done | bytes 29360144 | tf_op jit(solution)/shard_map/all_gather | solution.py:36
  441.5 22.6 %fusion.4 = bf16[448,4096]{1,0:T(8,128)(2,1)S(1)} fusion(bf16[3584,448]{1,0:T(8,128)(2,1)} %all-gather.4.cloned.1.call-done, bf16[1,4096,3584]{2,1,0:T(8,128)(2,1)} %all-gather.6.cloned.1.call-done), kind=kOutput, calls=%fused_computation.6 | convolution fusion | flops 13155172352 | bytes 36241408 | tf_op jit(solution)/shard_map/dot_general | solution.py:35
  464.2 2.2 copy.19
  466.4 4.5 all-to-all-start
  470.9 5.9 %copy.12 = bf16[1,256,7168]{1,2,0:T(8,128)(2,1)} copy(bf16[1,256,7168]{2,1,0:T(8,128)(2,1)} %param.11) | data formatting | bytes 7340032 | tf_op args[5]
  476.8 39.6 %all-to-all-done = bf16[16,256,448]{1,2,0:T(8,128)(2,1)} async-done(((bf16[16,256,448]{1,2,0:T(8,128)(2,1)}), bf16[16,256,448]{1,2,0:T(8,128)(2,1)}, u32[]{:S(2)}, u32[]{:S(2)}) %all-to-all-start) | async-done | bytes 3670048 | tf_op jit(solution)/shard_map/all_to_all | solution.py:40
  516.5 0.0 copy-start
  516.5 3.0 convert_element_type.60
  519.4 0.2 copy-done
  519.6 3.0 fusion.2
  522.6 5.9 %copy.14 = bf16[1,256,7168]{2,1,0:T(8,128)(2,1)} copy(bf16[1,256,7168]{1,2,0:T(8,128)(2,1)} %fusion.2) | data formatting | bytes 7340032
  (1 shorter events, 0.0 us)
Async XLA Ops:
  7.2 8.1 %copy-start.3 = (s32[1,28,448]{2,0,1:T(1,128)S(1)}, s32[1,28,448]{2,0,1:T(1,128)}, u32[]{:S(2)}) copy-start(s32[1,28,448]{2,0,1:T(1,128)} %param.7) | copy-start | bytes 150532
  7.2 181.0 %all-reduce.2.cloned.1.call-start = ((), (), s32[]{:S(2)}) async-start(), calls=%async_computation.1 | async-start | bytes 7340032 | tf_op jit(solution)/shard_map/psum | solution.py:28
  21.5 166.6 %copy-start.1 = (f32[448,448]{1,0:T(8,128)S(1)}, f32[448,448]{1,0:T(8,128)}, u32[]{:S(2)}) copy-start(f32[448,448]{1,0:T(8,128)} %param.8) | copy-start | bytes 2408452
  21.5 166.6 %copy-start.2 = (f32[448,448]{1,0:T(8,128)S(1)}, f32[448,448]{1,0:T(8,128)}, u32[]{:S(2)}) copy-start(f32[448,448]{1,0:T(8,128)} %param.9) | copy-start | bytes 2408452
  21.5 250.5 %all-gather.4.cloned.1.call-start = ((), (), s32[]{:S(2)}) async-start(), calls=%async_computation.2 | async-start | bytes 4128768 | tf_op jit(solution)/shard_map/all_gather | solution.py:34
  190.9 250.6 %all-gather.6.cloned.1.call-start = ((), (), s32[]{:S(2)}) async-start(), calls=%async_computation.3 | async-start | bytes 31195136 | tf_op jit(solution)/shard_map/all_gather | solution.py:36
  466.4 50.1 %all-to-all-start = ((bf16[16,256,448]{1,2,0:T(8,128)(2,1)}), bf16[16,256,448]{1,2,0:T(8,128)(2,1)}, u32[]{:S(2)}, u32[]{:S(2)}) async-start(bf16[16,256,448]{1,2,0:T(8,128)(2,1)} %bitcast.28), calls=%async_computation | async-start | bytes 7340032 | tf_op jit(solution)/shard_map/all_to_all | solution.py:40
  516.5 3.1 copy-start
Sparse Core Ops, SparseCore 0:
  21.6 166.4 all-reduce.1
  191.0 80.9 all-gather.3
  274.5 166.9 all-gather.5
where the time goes:
time: 536 us; the launch traced here: 535 us
  waiting for transfers between devices  457 us (85%)
  matrix products  22.6 us (4%)
  local copies, waits for them, and re-layouts  22.2 us (4%)
  other arithmetic  14.9 us (3%)
  between operations  13.8 us (3%)
    all_gather x1, waiting for transfers between devices, shards(): lax.all_gather(attention[0], 'fsdp', axis=0, tiled=True)  170 us
    psum x1, waiting for transfers between devices, shards(): lax.psum(delta_values.astype(jnp.bfloat16), 'replica').astype(jnp.float32)  167 us
    all_gather x1, waiting for transfers between devices, shards(): out_weight = lax.all_gather(out_block, 'replica', axis=0, tiled=True)  80.4 us
    all_to_all x1, waiting for transfers between devices, shards(): lax.all_to_all(columns, 'fsdp', split_axis=0, concat_axis=1, tiled=True)  39.6 us
    dot_general x1, matrix products, shards(): jnp.dot(lax.all_gather(attention[0], 'fsdp', axis=0, tiled=True), out_wei...  22.6 us
    unnamed x12, local copies, waits for them, and re-layouts  20 us
  transfers between devices with their start and end apart: 4, of which 4 were waited for; matrix products, arithmetic and copies ran while one was open for 1% of the time, Pallas kernels for 0%

commit v1 on v0

v1 whole, which is shorter than its diff:
```python
import jax
import jax.numpy as jnp
from jax import lax
from jax.experimental import pallas as pl
from jax.experimental.pallas import tpu as pltpu
from jax.sharding import PartitionSpec as P

MESH = pl.DeviceIdType.MESH
F32, BF16 = jnp.float32, jnp.bfloat16

COLS = 448
KDIM = 3584
TOK = 256
PAIR = 896
PIECE = 224
SEND = 7 * PIECE


def scale_of(exponents):
    scales = jnp.zeros(exponents.shape, F32)
    for exponent_value in range(-10, -5):
        scales = scales + jnp.where(
            exponents == exponent_value, jnp.float32(2.0**exponent_value), jnp.float32(0.0)
        )
    return scales


def device(x, y, z, c):
    return (z * 2 + lax.rem(x, 2), (y * 2 + x // 2) * 2 + c)


def kernel(
    codes, scales, params, momentum, attention,
    params_out, momentum_out, projected,
    codes_v, deltas, received, par_v, mom_v, summed, block, block_in, weight, att, outs,
    local_sem, rs_s, rs_r, at_s, at_r, sw_s, sw_r, sib_s, sib_r, xs, xr, zs, zr, os_, or_,
):
    r = lax.axis_index("replica")
    f = lax.axis_index("fsdp")
    z, xl = r // 2, lax.rem(r, 2)
    y, xh, c = f // 4, lax.rem(f // 2, 2), lax.rem(f, 2)
    x = xh * 2 + xl
    xo = lax.rem(x + 3 + 2 * xl, 4)
    x2 = lax.rem(x + 2, 4)
    xp = xh * 2 + (1 - xl)
    zu, zd, z2 = lax.rem(z + 1, 4), lax.rem(z + 3, 4), lax.rem(z + 2, 4)
    yu, yd = lax.rem(y + 1, 4), lax.rem(y + 3, 4)
    sibling = device(x, y, z, 1 - c)
    to_xp, to_xo = device(xp, y, z, c), device(xo, y, z, c)
    to_zu, to_zd = device(x, y, zu, c), device(x, y, zd, c)
    to_yu, to_yd = device(x, yu, z, c), device(x, yd, z, c)

    barrier = pltpu.get_barrier_semaphore()
    partners = [sibling, to_xo, to_yu, to_yd, device(x, lax.rem(y + 2, 4), z, c), to_xp]
    for dz in (1, 2, 3):
        for there in (x, xp):
            partners.append(device(there, y, lax.rem(z + dz, 4), c))
    for partner in partners:
        pl.semaphore_signal(barrier, inc=1, device_id=partner, device_id_type=MESH)

    z_order = [z2, zu, zd, z]
    code_copies = []
    for i, zz in enumerate(z_order):
        copy = pltpu.make_async_copy(
            codes.at[:, pl.ds(pl.multiple_of(zz * PAIR, 128), PAIR)], codes_v.at[i], local_sem.at[i]
        )
        copy.start()
        code_copies.append(copy)
    par_copy = pltpu.make_async_copy(params, par_v, local_sem.at[4])
    mom_copy = pltpu.make_async_copy(momentum, mom_v, local_sem.at[5])
    att_copy = pltpu.make_async_copy(attention, att.at[y], local_sem.at[6])
    par_copy.start()
    mom_copy.start()
    att_copy.start()
    pl.semaphore_wait(barrier, len(partners))

    pending = []

    def send(src, dst, s, q, to):
        copy = pltpu.make_async_remote_copy(
            src_ref=src, dst_ref=dst, send_sem=s, recv_sem=q, device_id=to, device_id_type=MESH
        )
        copy.start()
        pending.append(copy)
        return copy

    half = TOK // 2
    low, high = pl.ds(0, half), pl.ds(half, half)
    at0 = send(attention.at[low], att.at[y, low], at_s.at[0], at_r.at[0], to_yu)
    at1 = send(attention.at[high], att.at[y, high], at_s.at[1], at_r.at[1], to_yd)

    lane = lax.broadcasted_iota(jnp.int32, (PIECE, 128), 1) < 64
    rs = []
    for i, zz in enumerate(z_order):
        code_copies[i].wait()
        scale = scales[zz]

        def tile(t):
            return codes_v[i, :, 128 * t : 128 * (t + 1)].astype(F32) * scale[:, t : t + 1]

        for t in range(3):
            deltas[2 * zz, t * COLS : (t + 1) * COLS] = tile(t).astype(BF16)
            deltas[2 * zz + 1, t * COLS : (t + 1) * COLS] = tile(t + 4).astype(BF16)
        mid = tile(3)
        turned = pltpu.roll(mid, 64, 1)
        top, bottom = mid[:PIECE], mid[PIECE:]
        deltas[2 * zz, 3 * COLS :] = jnp.where(lane, top, turned[PIECE:]).astype(BF16)
        deltas[2 * zz + 1, 3 * COLS :] = jnp.where(lane, turned[:PIECE], bottom).astype(BF16)
        for j, there in enumerate((xp, x)):
            if i == 3 and j == 1:
                continue
            k = 2 * i + j
            to = device(there, y, zz, c)
            rs.append(
                send(deltas.at[2 * zz + lax.rem(there, 2)], received.at[k], rs_s.at[k], rs_r.at[k], to)
            )

    att_copy.wait()
    at0.wait_recv()
    at2 = send(att.at[yd, low], att.at[yd, low], at_s.at[2], at_r.at[2], to_yu)
    at3 = send(att.at[y, high], att.at[y, high], at_s.at[3], at_r.at[3], to_yu)
    at1.wait_recv()
    at4 = send(att.at[yu, high], att.at[yu, high], at_s.at[4], at_r.at[4], to_yd)
    at5 = send(att.at[y, low], att.at[y, low], at_s.at[5], at_r.at[5], to_yd)

    for copy in rs:
        copy.wait_recv()

    def total(rows, size):
        acc = deltas[r, pl.ds(rows, size)].astype(F32)
        for k in range(7):
            acc = acc + received[k, pl.ds(rows, size)].astype(F32)
        return acc

    fill = jnp.zeros((64, 128), F32)
    for t in range(3):
        piece = jnp.concatenate([total(t * COLS, COLS), fill], axis=0).T
        summed[pl.ds(pl.multiple_of(xl * 64 + t * 128, 64), 128)] = piece[:, :COLS]
    packed = total(3 * COLS, PIECE)
    piece = jnp.concatenate([packed, pltpu.roll(packed, 64, 1), fill], axis=0).T
    summed[pl.ds(pl.multiple_of((1 - xl) * 384, 64), 64)] = piece[:64, :COLS]

    par_copy.wait()
    mom_copy.wait()
    outer_grad = summed[...] / 8
    new_momentum = 0.9 * mom_v[...] + outer_grad
    new_params = par_v[...] - 0.7 * (outer_grad + 0.9 * new_momentum)
    mom_v[...] = new_momentum
    par_v[...] = new_params
    block[...] = jnp.concatenate(
        [new_params, jnp.zeros((COLS, 64), F32)], axis=1
    ).astype(BF16)
    away = pl.ds(pl.multiple_of((1 - c) * PIECE, 16), PIECE)
    keep = pl.ds(pl.multiple_of(c * PIECE, 16), PIECE)
    swap = send(block.at[away], block_in, sw_s, sw_r, sibling)
    par_save = pltpu.make_async_copy(par_v, params_out, local_sem.at[4])
    mom_save = pltpu.make_async_copy(mom_v, momentum_out, local_sem.at[5])
    par_save.start()
    mom_save.start()
    swap.wait_recv()
    mine, other = block[keep].astype(F32), block_in[...].astype(F32)
    first = c == 0
    left = jnp.where(first, mine, other)
    right = pltpu.roll(jnp.where(first, other, mine), 64, 1)
    seam = jnp.where(lane, left[:, 384:], right[:, :128])
    own_rows = pl.ds(pl.multiple_of(r * COLS + c * PIECE, 16), PIECE)
    weight[xh, own_rows, :384] = left[:, :384].astype(BF16)
    weight[xh, own_rows, 384:512] = seam.astype(BF16)
    weight[xh, own_rows, 512:] = right[:, 128:].astype(BF16)

    def unit(x_, z_, part, lo=0, size=112):
        start = (2 * z_ + lax.rem(x_, 2)) * COLS + c * PIECE + part * 112 + lo
        return weight.at[x_ // 2, pl.ds(pl.multiple_of(start, 16), size)]

    shares = []

    def share(ref):
        k = len(shares)
        shares.append(send(ref, ref, sib_s.at[k], sib_r.at[k], sibling))
        return shares[-1]

    n_x, n_z = [0], [0]

    def along_x(ref, to):
        k = n_x[0]
        n_x[0] += 1
        return send(ref, ref, xs.at[k], xr.at[k], to)

    def along_z(ref, to):
        k = n_z[0]
        n_z[0] += 1
        return send(ref, ref, zs.at[k], zr.at[k], to)

    XP, XO, ZU, ZD = to_xp, to_xo, to_zu, to_zd
    own_shares, late_shares = [], []
    pz_u = along_z(unit(x, z, 0), ZU)
    pz_d = along_z(unit(x, z, 0), ZD)
    qx_p = along_x(unit(x, z, 1), XP)
    qx_o = along_x(unit(x, z, 1), XO)
    z_units = [z, zd, zu, z2]
    x_units = [x, xp, xo, x2]
    px_p, px_o, qz_u, qz_d = [], [], [], []
    px_p.append(along_x(unit(x, z, 0), XP))
    px_o.append(along_x(unit(x, z, 0), XO))
    qz_u.append(along_z(unit(x, z, 1), ZU))
    qz_d.append(along_z(unit(x, z, 1), ZD))
    own_shares.append(share(weight.at[xh, own_rows]))

    pz_u.wait_recv()
    pz2_u = along_z(unit(x, zd, 0, 0, 64), ZU)
    px_p.append(along_x(unit(x, zd, 0), XP))
    px_o.append(along_x(unit(x, zd, 0), XO))
    own_shares.append(share(unit(x, zd, 0)))
    pz_d.wait_recv()
    pz2_d = along_z(unit(x, zu, 0, 64, 48), ZD)
    px_p.append(along_x(unit(x, zu, 0), XP))
    px_o.append(along_x(unit(x, zu, 0), XO))
    own_shares.append(share(unit(x, zu, 0)))
    qx_p.wait_recv()
    qx2_o = along_x(unit(xp, z, 1, 0, 64), XO)
    qz_u.append(along_z(unit(xp, z, 1), ZU))
    qz_d.append(along_z(unit(xp, z, 1), ZD))
    own_shares.append(share(unit(xp, z, 1)))
    qx_o.wait_recv()
    qx2_p = along_x(unit(xo, z, 1, 64, 48), XP)
    qz_u.append(along_z(unit(xo, z, 1), ZU))
    qz_d.append(along_z(unit(xo, z, 1), ZD))
    late_shares.append(share(unit(xo, z, 1)))
    pz2_u.wait_recv()
    pz2_d.wait_recv()
    px_p.append(along_x(unit(x, z2, 0), XP))
    px_o.append(along_x(unit(x, z2, 0), XO))
    own_shares.append(share(unit(x, z2, 0)))
    qx2_o.wait_recv()
    qx2_p.wait_recv()
    qz_u.append(along_z(unit(x2, z, 1), ZU))
    qz_d.append(along_z(unit(x2, z, 1), ZD))
    late_shares.append(share(unit(x2, z, 1)))

    qz2 = [None] * 4

    def pass_z(j, bucket):
        qz_u[j].wait_recv()
        if j in (0, 2):
            qz2[j] = along_z(unit(x_units[j], zd, 1), ZU)
        bucket.append(share(unit(x_units[j], zd, 1)))
        qz_d[j].wait_recv()
        if j in (1, 3):
            qz2[j] = along_z(unit(x_units[j], zu, 1), ZD)
        bucket.append(share(unit(x_units[j], zu, 1)))

    px2 = [None] * 4
    pass_z(0, own_shares)
    pass_z(1, own_shares)
    for j in range(4):
        px_p[j].wait_recv()
        if j in (0, 1):
            px2[j] = along_x(unit(xp, z_units[j], 0), XO)
        own_shares.append(share(unit(xp, z_units[j], 0)))
        px_o[j].wait_recv()
        if j in (2, 3):
            px2[j] = along_x(unit(xo, z_units[j], 0), XP)
        late_shares.append(share(unit(xo, z_units[j], 0)))
    for j in (0, 1):
        qz2[j].wait_recv()
        own_shares.append(share(unit(x_units[j], z2, 1)))
    for copy in own_shares:
        copy.wait_recv()

    for copy in (at2, at3, at4, at5):
        copy.wait_recv()

    def multiply(side, begin, end):
        columns = xh if side == 0 else 1 - xh
        place = pl.ds(pl.multiple_of(y * 1792 + columns * PAIR, 128), PAIR)

        def step(i, carry):
            yy = lax.rem(y + 2 + i * (i + 1) // 2, 4)
            outs[side, i] = jnp.dot(
                att[yy], weight[columns], preferred_element_type=F32
            ).astype(BF16)

            @pl.when(i < 3)
            def _():
                pltpu.make_async_remote_copy(
                    src_ref=outs.at[side, i],
                    dst_ref=projected.at[:, place],
                    send_sem=os_.at[side, i],
                    recv_sem=or_.at[side, i],
                    device_id=device(x, yy, z, c),
                    device_id_type=MESH,
                ).start()

            @pl.when(i == 3)
            def _():
                pltpu.make_async_copy(
                    outs.at[side, i], projected.at[:, place], os_.at[side, i]
                ).start()

            return carry

        lax.fori_loop(begin, end, step, 0)
        return place

    place0 = multiply(0, 0, 2)
    pass_z(2, late_shares)
    pass_z(3, late_shares)
    multiply(0, 2, 4)
    for j in (0, 1, 2, 3):
        px2[j].wait_recv()
        late_shares.append(share(unit(x2, z_units[j], 0)))
    for j in (2, 3):
        qz2[j].wait_recv()
        late_shares.append(share(unit(x_units[j], z2, 1)))
    for copy in late_shares:
        copy.wait_recv()
    place1 = multiply(1, 0, 4)

    for copy in pending:
        copy.wait_send()
    par_save.wait()
    mom_save.wait()
    for side, place in ((0, place0), (1, place1)):
        pltpu.make_async_copy(outs.at[side, 3], projected.at[:, place], os_.at[side, 3]).wait()
        for i in range(3):
            out = pltpu.make_async_remote_copy(
                src_ref=outs.at[side, i],
                dst_ref=projected.at[:, place],
                send_sem=os_.at[side, i],
                recv_sem=or_.at[side, i],
                device_id=to_yu,
                device_id_type=MESH,
            )
            out.wait_send()
            out.wait_recv()


def shards(codes, exponents, params, momentum, attention, residual):
    scales = scale_of(exponents[0]).T.reshape(COLS, 4, 7).transpose(1, 0, 2)
    any_space = pl.BlockSpec(memory_space=pl.ANY)
    vmem = pl.BlockSpec(memory_space=pltpu.VMEM)
    dma = pltpu.SemaphoreType.DMA
    new_params, new_momentum, projected = pl.pallas_call(
        kernel,
        out_shape=(
            jax.ShapeDtypeStruct((COLS, COLS), F32),
            jax.ShapeDtypeStruct((COLS, COLS), F32),
            jax.ShapeDtypeStruct((TOK, 4 * 2 * PAIR), BF16),
        ),
        in_specs=[any_space, vmem, any_space, any_space, any_space],
        out_specs=(any_space, any_space, any_space),
        scratch_shapes=[
            pltpu.VMEM((4, COLS, PAIR), jnp.int32),
            pltpu.VMEM((8, SEND, 128), BF16),
            pltpu.VMEM((7, SEND, 128), BF16),
            pltpu.VMEM((COLS, COLS), F32),
            pltpu.VMEM((COLS, COLS), F32),
            pltpu.VMEM((COLS, COLS), F32),
            pltpu.VMEM((COLS, 512), BF16),
            pltpu.VMEM((PIECE, 512), BF16),
            pltpu.VMEM((2, KDIM, PAIR), BF16),
            pltpu.VMEM((4, TOK, KDIM), BF16),
            pltpu.VMEM((2, 4, TOK, PAIR), BF16),
            dma((7,)),
            dma((7,)), dma((7,)),
            dma((6,)), dma((6,)),
            dma, dma,
            dma((31,)), dma((31,)),
            dma((16,)), dma((16,)),
            dma((16,)), dma((16,)),
            dma((2, 4)), dma((2, 4)),
        ],
        compiler_params=pltpu.CompilerParams(
            collective_id=0, has_side_effects=True, vmem_limit_bytes=60 * 2**20
        ),
    )(jnp.swapaxes(codes[0], 0, 1), scales, params, momentum, attention[0])
    hidden_out = (residual[0].astype(F32) + projected.astype(F32)).astype(BF16)
    return (new_params, new_momentum, hidden_out[None])


def solution(mesh):
    placed = (
        P("replica", None, "fsdp"),
        P("replica", None, "fsdp"),
        P("replica", "fsdp"),
        P("replica", "fsdp"),
        P("replica", "fsdp", None),
        P("replica", "fsdp", None),
    )
    return jax.shard_map(
        shards,
        mesh=mesh,
        in_specs=placed,
        out_specs=(P("replica", "fsdp"), P("replica", "fsdp"), P("replica", "fsdp", None)),
        check_vma=False,
    )
```

time: 536 us -> 140 us (0.26)
  waiting for transfers between devices: 457 us -> 0 us
  Pallas kernels: 0 us -> 129 us
  matrix products: 22.6 us -> 0 us
  local copies, waits for them, and re-layouts: 22.2 us -> 3.14 us
  between operations: 13.8 us -> 0.68 us
  other arithmetic: 14.9 us -> 6.39 us
    all_gather x2 -> x0, waiting for transfers between devices: 250 us -> none  [the longest x1 170 us: shards(): lax.all_gather(attention[0], 'fsdp', axis=0, tiled=True)]
    psum x1 -> x0, waiting for transfers between devices: 167 us -> none  [shards(): lax.psum(delta_values.astype(jnp.bfloat16), 'replica').astype(jnp.float32)]
    pallas_call x0 -> x1, Pallas kernels: none -> 129 us  [shards(): pl.pallas_call(kernel, out_shape=(jax.ShapeDtypeStruct((COLS, COLS), F32)...]
    all_to_all x1 -> x0, waiting for transfers between devices: 39.6 us -> none  [shards(): lax.all_to_all(columns, 'fsdp', split_axis=0, concat_axis=1, tiled=True)]
    dot_general x1 -> x0, matrix products: 22.6 us -> none  [shards(): jnp.dot(lax.all_gather(attention[0], 'fsdp', axis=0, tiled=True), out_wei...]
    unnamed x12 -> x9, local copies, waits for them, and re-layouts: 20 us -> 1.86 us
    convert_element_type x4 -> x0, other arithmetic: 14.7 us -> none  [the longest x1 6.01 us: shards(): delta_values.astype(jnp.bfloat16)]
    broadcast_in_dim x0 -> x1, other arithmetic: none -> 5.36 us  [shards(): return (new_params, new_momentum, hidden_out[None])]
  transfers between devices with their start and end apart: 4 -> 0, of which waited for: 4 -> 0; matrix products, arithmetic and copies ran while one was open for 1% -> 0% of each run, Pallas kernels for 0% -> 0%
where the time goes in v1:
time: 140 us; the launch traced here: 139 us
  Pallas kernels  129 us (92%)
  other arithmetic  6.39 us (5%)
  local copies, waits for them, and re-layouts  3.14 us (2%)
    pallas_call x1, Pallas kernels, shards(): pl.pallas_call(kernel, out_shape=(jax.ShapeDtypeStruct((COLS, COLS), F32)...  129 us
    broadcast_in_dim x1, other arithmetic, shards(): return (new_params, new_momentum, hidden_out[None])  5.36 us

profile of v1, /device:TPU:1, one launch (start us, length us, event | category | flops | bytes accessed | tf_op | source)
XLA Modules:
  0.0 139.4 jit_solution(18326710013340197043)
XLA Ops:
  0.6 1.0 fusion.5
  1.7 1.3 copy.9
  3.0 0.0 copy-start
  3.0 129.2 %shard_map.85 = (f32[448,448]{1,0:T(8,128)}, f32[448,448]{1,0:T(8,128)}, bf16[256,7168]{1,0:T(8,128)(2,1)}) custom-call(s32[448,3584]{1,0:T(8,128)} %bitcast.17, f32[4,448,7]{2,1,0:T(8,128)} %bitcast.18, f32[448,448]{1,0:T(8,128)} %params.1, f32[448,448]{1,0:T(8,128)} %momentum.1, bf16[256,3584]{1,0:T(8,128)(2,1)} %bitcast.19), custom_call_target="tpu_custom_call" | custom-call | tf_op jit(solution)/shard_map/pallas_call | solution.py:343
  132.1 0.0 copy-done
  132.2 0.0 copy-start.2
  132.2 0.0 copy-start.1
  132.2 5.4 %fusion.1 = bf16[1,256,7168]{2,1,0:T(8,128)(2,1)} fusion(bf16[256,7168]{1,0:T(8,128)(2,1)} %get-tuple-element.8, bf16[1,256,7168]{2,1,0:T(8,128)(2,1)S(1)} %copy-done), kind=kLoop, calls=%fused_computation.2 | loop fusion | flops 7340032 | bytes 11010048 | tf_op jit(solution)/shard_map/broadcast_in_dim | solution.py:378
  137.5 0.0 copy-done.2
  137.5 0.9 copy.15
  138.5 0.0 copy-done.1
  138.5 0.9 copy.16
  (2 shorter events, 0.0 us)
Async XLA Ops:
  3.0 129.2 %copy-start = (bf16[1,256,7168]{2,1,0:T(8,128)(2,1)S(1)}, bf16[1,256,7168]{2,1,0:T(8,128)(2,1)}, u32[]{:S(2)}) copy-start(bf16[1,256,7168]{2,1,0:T(8,128)(2,1)} %param.11) | copy-start | bytes 11010052
  132.2 5.4 %copy-start.2 = (f32[448,448]{1,0:T(8,128)S(1)}, f32[448,448]{1,0:T(8,128)}, u32[]{:S(2)}) copy-start(f32[448,448]{1,0:T(8,128)} %get-tuple-element.12) | copy-start | bytes 2408452
  132.2 6.3 %copy-start.1 = (f32[448,448]{1,0:T(8,128)S(1)}, f32[448,448]{1,0:T(8,128)}, u32[]{:S(2)}) copy-start(f32[448,448]{1,0:T(8,128)} %get-tuple-element.13) | copy-start | bytes 2408452

commit v2 on v1

v2 whole, which is shorter than its diff:
```python
import jax
import jax.numpy as jnp
from jax import lax
from jax.experimental import pallas as pl
from jax.experimental.pallas import tpu as pltpu
from jax.sharding import PartitionSpec as P

MESH = pl.DeviceIdType.MESH
F32, BF16 = jnp.float32, jnp.bfloat16

COLS = 448
KDIM = 3584
TOK = 256
PAIR = 896
PIECE = 224
SEND = 7 * PIECE
VMEM_LIMIT = 48 * 2**20


def keep(array):
    return pltpu.with_memory_space_constraint(array, pltpu.HBM)


def scale_of(exponents):
    scales = jnp.zeros(exponents.shape, F32)
    for exponent_value in range(-10, -5):
        scales = scales + jnp.where(
            exponents == exponent_value, jnp.float32(2.0**exponent_value), jnp.float32(0.0)
        )
    return scales


def device(x, y, z, c):
    return (z * 2 + lax.rem(x, 2), (y * 2 + x // 2) * 2 + c)


def kernel(
    codes, exponents, params, momentum, attention, residual,
    params_out, momentum_out, hidden_out,
    codes_v, exp_v, deltas, received, par_v, mom_v, summed, block, block_in, weight, att, outs, got, hid,
    local_sem, rs_s, rs_r, at_s, at_r, sw_s, sw_r, sib_s, sib_r, xs, xr, zs, zr, os_, or_, save_sem,
):
    r = lax.axis_index("replica")
    f = lax.axis_index("fsdp")
    z, xl = r // 2, lax.rem(r, 2)
    y, xh, c = f // 4, lax.rem(f // 2, 2), lax.rem(f, 2)
    x = xh * 2 + xl
    xo = lax.rem(x + 3 + 2 * xl, 4)
    x2 = lax.rem(x + 2, 4)
    xp = xh * 2 + (1 - xl)
    zu, zd, z2 = lax.rem(z + 1, 4), lax.rem(z + 3, 4), lax.rem(z + 2, 4)
    yu, yd = lax.rem(y + 1, 4), lax.rem(y + 3, 4)
    sibling = device(x, y, z, 1 - c)
    to_xp, to_xo = device(xp, y, z, c), device(xo, y, z, c)
    to_zu, to_zd = device(x, y, zu, c), device(x, y, zd, c)
    to_yu, to_yd = device(x, yu, z, c), device(x, yd, z, c)

    barrier = pltpu.get_barrier_semaphore()
    partners = [sibling, to_xp, to_xo, to_yu, to_yd, device(x, lax.rem(y + 2, 4), z, c)]
    partners += [to_zu, to_zd, device(x, y, z2, c)]
    for partner in partners:
        pl.semaphore_signal(barrier, inc=1, device_id=partner, device_id_type=MESH)

    z_order = [z2, zu, zd, z]
    exp_copy = pltpu.make_async_copy(exponents, exp_v, local_sem.at[8])
    exp_copy.start()
    code_copies = []
    for i, zz in enumerate(z_order):
        copy = pltpu.make_async_copy(
            codes.at[:, pl.ds(pl.multiple_of(zz * PAIR, 128), PAIR)], codes_v.at[i], local_sem.at[i]
        )
        copy.start()
        code_copies.append(copy)
    par_copy = pltpu.make_async_copy(params, par_v, local_sem.at[4])
    mom_copy = pltpu.make_async_copy(momentum, mom_v, local_sem.at[5])
    att_copy = pltpu.make_async_copy(attention, att.at[y], local_sem.at[6])
    res_copy = pltpu.make_async_copy(residual, hid, local_sem.at[7])
    par_copy.start()
    mom_copy.start()
    att_copy.start()
    res_copy.start()
    pl.semaphore_wait(barrier, len(partners))

    pending = []

    def send(src, dst, s, q, to):
        copy = pltpu.make_async_remote_copy(
            src_ref=src, dst_ref=dst, send_sem=s, recv_sem=q, device_id=to, device_id_type=MESH
        )
        copy.start()
        pending.append(copy)
        return copy

    half = TOK // 2
    low, high = pl.ds(0, half), pl.ds(half, half)
    at0 = send(attention.at[low], att.at[y, low], at_s.at[0], at_r.at[0], to_yu)
    at1 = send(attention.at[high], att.at[y, high], at_s.at[1], at_r.at[1], to_yd)
    at3 = send(attention.at[high], att.at[y, high], at_s.at[3], at_r.at[3], to_yu)
    at5 = send(attention.at[low], att.at[y, low], at_s.at[5], at_r.at[5], to_yd)

    lane = lax.broadcasted_iota(jnp.int32, (PIECE, 128), 1) < 64
    rs, other = [], 1 - xl
    exp_copy.wait()
    for i, zz in enumerate(z_order):
        code_copies[i].wait()
        scale = [scale_of(exp_v[7 * zz + t]) for t in range(7)]
        scale = jnp.concatenate(scale + [jnp.zeros((1, COLS), F32)], axis=0)
        scale = jnp.concatenate([scale, jnp.zeros((8, 64), F32)], axis=1).T[:COLS]

        def tile(t):
            return codes_v[i, :, 128 * t : 128 * (t + 1)].astype(F32) * scale[:, t : t + 1]

        for t in range(3):
            deltas[2 * zz, t * COLS : (t + 1) * COLS] = tile(t).astype(BF16)
            deltas[2 * zz + 1, t * COLS : (t + 1) * COLS] = tile(t + 4).astype(BF16)
        mid = tile(3)
        turned = pltpu.roll(mid, 64, 1)
        top, bottom = mid[:PIECE], mid[PIECE:]
        deltas[2 * zz, 3 * COLS :] = jnp.where(lane, top, turned[PIECE:]).astype(BF16)
        deltas[2 * zz + 1, 3 * COLS :] = jnp.where(lane, turned[:PIECE], bottom).astype(BF16)
        if i == 0:
            pair = send(deltas.at[2 * zz + other], received.at[0], rs_s.at[0], rs_r.at[0], to_xp)
        elif i < 3:
            to = device(x, y, zz, c)
            rs.append(send(deltas.at[2 * zz + other], received.at[i], rs_s.at[i], rs_r.at[i], to))
            k = i + 2
            rs.append(send(deltas.at[2 * zz + xl], received.at[k], rs_s.at[k], rs_r.at[k], to))

    def add(place, slots):
        acc = deltas[place].astype(F32)
        for k in slots:
            acc = acc + received[k].astype(F32)
        deltas[place] = acc.astype(BF16)

    far, near = 2 * z2 + xl, 2 * z + other
    pair.wait_recv()
    add(far, (0,))
    rs.append(send(deltas.at[far], received.at[5], rs_s.at[5], rs_r.at[5], device(x, y, z2, c)))
    rs[0].wait_recv()
    rs[2].wait_recv()
    add(near, (1, 2))
    rs.append(send(deltas.at[near], received.at[6], rs_s.at[6], rs_r.at[6], to_xp))

    att_copy.wait()
    at0.wait_recv()
    at2 = send(att.at[yd, low], att.at[yd, low], at_s.at[2], at_r.at[2], to_yu)
    at1.wait_recv()
    at4 = send(att.at[yu, high], att.at[yu, high], at_s.at[4], at_r.at[4], to_yd)

    for copy in (rs[1], rs[3], rs[4], rs[5]):
        copy.wait_recv()

    def total(rows, size):
        acc = deltas[r, pl.ds(rows, size)].astype(F32)
        for k in range(3, 7):
            acc = acc + received[k, pl.ds(rows, size)].astype(F32)
        return acc

    fill = jnp.zeros((64, 128), F32)
    for t in range(3):
        piece = jnp.concatenate([total(t * COLS, COLS), fill], axis=0).T
        summed[pl.ds(pl.multiple_of(xl * 64 + t * 128, 64), 128)] = piece[:, :COLS]
    packed = total(3 * COLS, PIECE)
    piece = jnp.concatenate([packed, pltpu.roll(packed, 64, 1), fill], axis=0).T
    summed[pl.ds(pl.multiple_of((1 - xl) * 384, 64), 64)] = piece[:64, :COLS]

    par_copy.wait()
    mom_copy.wait()
    outer_grad = summed[...] / 8
    new_momentum = 0.9 * mom_v[...] + outer_grad
    new_params = par_v[...] - 0.7 * (outer_grad + 0.9 * new_momentum)
    mom_v[...] = new_momentum
    par_v[...] = new_params
    block[...] = jnp.concatenate(
        [new_params, jnp.zeros((COLS, 64), F32)], axis=1
    ).astype(BF16)
    away = pl.ds(pl.multiple_of((1 - c) * PIECE, 16), PIECE)
    keep = pl.ds(pl.multiple_of(c * PIECE, 16), PIECE)
    swap = send(block.at[away], block_in, sw_s, sw_r, sibling)
    par_save = pltpu.make_async_copy(par_v, params_out, local_sem.at[4])
    mom_save = pltpu.make_async_copy(mom_v, momentum_out, local_sem.at[5])
    par_save.start()
    mom_save.start()
    swap.wait_recv()
    mine, theirs = block[keep].astype(F32), block_in[...].astype(F32)
    first = c == 0
    left = jnp.where(first, mine, theirs)
    right = pltpu.roll(jnp.where(first, theirs, mine), 64, 1)
    seam = jnp.where(lane, left[:, 384:], right[:, :128])
    own_rows = pl.ds(pl.multiple_of(r * COLS + c * PIECE, 16), PIECE)
    weight[xh, own_rows, :384] = left[:, :384].astype(BF16)
    weight[xh, own_rows, 384:512] = seam.astype(BF16)
    weight[xh, own_rows, 512:] = right[:, 128:].astype(BF16)

    def unit(x_, z_, part, lo=0, size=112):
        start = (2 * z_ + lax.rem(x_, 2)) * COLS + c * PIECE + part * 112 + lo
        return weight.at[x_ // 2, pl.ds(pl.multiple_of(start, 16), size)]

    shares = []

    def share(ref):
        k = len(shares)
        shares.append(send(ref, ref, sib_s.at[k], sib_r.at[k], sibling))
        return shares[-1]

    n_x, n_z = [0], [0]

    def along_x(ref, to):
        k = n_x[0]
        n_x[0] += 1
        return send(ref, ref, xs.at[k], xr.at[k], to)

    def along_z(ref, to):
        k = n_z[0]
        n_z[0] += 1
        return send(ref, ref, zs.at[k], zr.at[k], to)

    XP, XO, ZU, ZD = to_xp, to_xo, to_zu, to_zd
    own_shares, late_shares = [], []
    pz_u = along_z(unit(x, z, 0), ZU)
    pz_d = along_z(unit(x, z, 0), ZD)
    qx_p = along_x(unit(x, z, 1), XP)
    qx_o = along_x(unit(x, z, 1), XO)
    z_units = [z, zd, zu, z2]
    x_units = [x, xp, xo, x2]
    px_p, px_o, qz_u, qz_d = [], [], [], []
    px_p.append(along_x(unit(x, z, 0), XP))
    px_o.append(along_x(unit(x, z, 0), XO))
    qz_u.append(along_z(unit(x, z, 1), ZU))
    qz_d.append(along_z(unit(x, z, 1), ZD))
    own_shares.append(share(weight.at[xh, own_rows]))

    def both(u, d, u_, d_):
        u.append(along_z(u_, ZU))
        d.append(along_z(d_, ZD))

    pz_u.wait_recv()
    pz2_u = along_z(unit(x, zd, 0, 0, 64), ZU)
    px_p.append(along_x(unit(x, zd, 0), XP))
    px_o.append(along_x(unit(x, zd, 0), XO))
    own_shares.append(share(unit(x, zd, 0)))
    pz_d.wait_recv()
    pz2_d = along_z(unit(x, zu, 0, 64, 48), ZD)
    px_p.append(along_x(unit(x, zu, 0), XP))
    px_o.append(along_x(unit(x, zu, 0), XO))
    own_shares.append(share(unit(x, zu, 0)))
    qx_p.wait_recv()
    both(qz_u, qz_d, unit(xp, z, 1), unit(xp, z, 1))
    own_shares.append(share(unit(xp, z, 1)))
    qx_o.wait_recv()
    late_shares.append(share(unit(xo, z, 1)))

    def got_z(j, bucket):
        qz_u[j].wait_recv()
        bucket.append(share(unit(x_units[j], zd, 1)))
        qz_d[j].wait_recv()
        bucket.append(share(unit(x_units[j], zu, 1)))

    def got_x(j):
        px_p[j].wait_recv()
        own_shares.append(share(unit(xp, z_units[j], 0)))
        px_o[j].wait_recv()
        late_shares.append(share(unit(xo, z_units[j], 0)))

    px2, qz2 = [None] * 4, [None] * 4
    got_z(0, own_shares)
    qz2[0] = along_z(unit(x, zd, 1), ZU)
    got_x(0)
    pz2_u.wait_recv()
    pz2_d.wait_recv()
    px_p.append(along_x(unit(x, z2, 0), XP))
    px_o.append(along_x(unit(x, z2, 0), XO))
    own_shares.append(share(unit(x, z2, 0)))
    qx2_o = along_x(unit(xp, z, 1, 0, 64), XO)
    qx2_p = along_x(unit(xo, z, 1, 64, 48), XP)
    got_x(1)
    px2[0] = along_x(unit(xp, z_units[0], 0), XO)
    px2[1] = along_x(unit(xp, z_units[1], 0), XO)
    got_z(1, own_shares)
    qz2[1] = along_z(unit(xp, zu, 1), ZD)
    both(qz_u, qz_d, unit(xo, z, 1), unit(xo, z, 1))
    got_x(2)
    px2[2] = along_x(unit(xo, z_units[2], 0), XP)
    for j in (0, 1):
        qz2[j].wait_recv()
        own_shares.append(share(unit(x_units[j], z2, 1)))
    got_x(3)
    px2[3] = along_x(unit(xo, z_units[3], 0), XP)
    for copy in own_shares:
        copy.wait_recv()

    for copy in (at2, at3, at4, at5):
        copy.wait_recv()

    def place(side, yy):
        columns = xh if side == 0 else 1 - xh
        return pl.ds(pl.multiple_of(yy * 1792 + columns * PAIR, 128), PAIR)

    def finish(side, i, value):
        here = place(side, lax.rem(y + 6 - i * (i + 1) // 2, 4))
        hid[:, here] = (hid[:, here].astype(F32) + value.astype(F32)).astype(BF16)
        pltpu.make_async_copy(
            hid.at[:, here], hidden_out.at[:, here], save_sem.at[side, i]
        ).start()

    def block_copy(side, i, to):
        return pltpu.make_async_remote_copy(
            src_ref=outs.at[side, i],
            dst_ref=got.at[side, i],
            send_sem=os_.at[side, i],
            recv_sem=or_.at[side, i],
            device_id=to,
            device_id_type=MESH,
        )

    def multiply(side, begin, end):
        columns = xh if side == 0 else 1 - xh

        def step(i, carry):
            yy = lax.rem(y + 2 + i * (i + 1) // 2, 4)
            result = jnp.dot(att[yy], weight[columns], preferred_element_type=F32).astype(BF16)

            @pl.when(i < 3)
            def _():
                outs[side, i] = result
                block_copy(side, i, device(x, yy, z, c)).start()

            @pl.when(i == 3)
            def _():
                finish(side, i, result)

            return carry

        lax.fori_loop(begin, end, step, 0)

    res_copy.wait()
    multiply(0, 0, 1)
    qx2_o.wait_recv()
    qx2_p.wait_recv()
    both(qz_u, qz_d, unit(x2, z, 1), unit(x2, z, 1))
    late_shares.append(share(unit(x2, z, 1)))
    got_z(2, late_shares)
    qz2[2] = along_z(unit(xo, zd, 1), ZU)
    multiply(0, 1, 3)
    got_z(3, late_shares)
    qz2[3] = along_z(unit(x2, zu, 1), ZD)
    multiply(0, 3, 4)
    for j in (0, 1, 2, 3):
        px2[j].wait_recv()
        late_shares.append(share(unit(x2, z_units[j], 0)))
    for j in (2, 3):
        qz2[j].wait_recv()
        late_shares.append(share(unit(x_units[j], z2, 1)))
    for copy in late_shares:
        copy.wait_recv()
    multiply(1, 0, 4)

    for side in range(2):

        def arrive(i, carry):
            block_copy(side, i, to_yu).wait_recv()
            finish(side, i, got[side, i])
            return carry

        lax.fori_loop(0, 3, arrive, 0)

    for copy in pending:
        copy.wait_send()
    par_save.wait()
    mom_save.wait()
    for side in range(2):
        for i in range(4):
            here = place(side, y)
            pltpu.make_async_copy(
                hid.at[:, here], hidden_out.at[:, here], save_sem.at[side, i]
            ).wait()
            if i < 3:
                block_copy(side, i, to_yu).wait_send()


def store(hidden, params, momentum, hidden_out, params_out, momentum_out, sem):
    copies = [
        pltpu.make_async_copy(params, params_out, sem.at[4]),
        pltpu.make_async_copy(momentum, momentum_out, sem.at[5]),
    ]
    for k in range(4):
        rows = pl.ds(k * TOK // 4, TOK // 4)
        copies.append(pltpu.make_async_copy(hidden.at[rows], hidden_out.at[rows], sem.at[k]))
    for copy in copies:
        copy.start()
    for copy in copies:
        copy.wait()


def shards(codes, exponents, params, momentum, attention, residual):
    any_space = pl.BlockSpec(memory_space=pl.ANY)
    dma = pltpu.SemaphoreType.DMA
    outer = jax.ShapeDtypeStruct((COLS, COLS), F32)
    hidden = jax.ShapeDtypeStruct((TOK, 4 * 2 * PAIR), BF16)
    new_params, new_momentum, new_hidden = pl.pallas_call(
        kernel,
        out_shape=(outer, outer, hidden),
        in_specs=[any_space] * 6,
        out_specs=(any_space, any_space, any_space),
        scratch_shapes=[
            pltpu.VMEM((4, COLS, PAIR), jnp.int32),
            pltpu.VMEM((4 * 7, 1, COLS), jnp.int32),
            pltpu.VMEM((8, SEND, 128), BF16),
            pltpu.VMEM((7, SEND, 128), BF16),
            pltpu.VMEM((COLS, COLS), F32),
            pltpu.VMEM((COLS, COLS), F32),
            pltpu.VMEM((COLS, COLS), F32),
            pltpu.VMEM((COLS, 512), BF16),
            pltpu.VMEM((PIECE, 512), BF16),
            pltpu.VMEM((2, KDIM, PAIR), BF16),
            pltpu.VMEM((4, TOK, KDIM), BF16),
            pltpu.VMEM((2, 3, TOK, PAIR), BF16),
            pltpu.VMEM((2, 3, TOK, PAIR), BF16),
            pltpu.VMEM((TOK, 4 * 2 * PAIR), BF16),
            dma((9,)),
            dma((7,)), dma((7,)),
            dma((6,)), dma((6,)),
            dma, dma,
            dma((31,)), dma((31,)),
            dma((16,)), dma((16,)),
            dma((16,)), dma((16,)),
            dma((2, 3)), dma((2, 3)),
            dma((2, 4)),
        ],
        compiler_params=pltpu.CompilerParams(
            collective_id=0, has_side_effects=True, vmem_limit_bytes=VMEM_LIMIT
        ),
    )(
        jnp.swapaxes(codes[0], 0, 1),
        keep(jnp.swapaxes(exponents, 0, 1)),
        *(keep(a) for a in (params, momentum, attention[0], residual[0])),
    )
    new_hidden, new_params, new_momentum = pl.pallas_call(
        store,
        out_shape=(hidden, outer, outer),
        in_specs=[any_space] * 3,
        out_specs=(any_space, any_space, any_space),
        scratch_shapes=[dma((6,))],
        compiler_params=pltpu.CompilerParams(vmem_limit_bytes=2**20),
    )(new_hidden, new_params, new_momentum)
    return (new_params, new_momentum, new_hidden[None])


def solution(mesh):
    placed = (
        P("replica", None, "fsdp"),
        P("replica", None, "fsdp"),
        P("replica", "fsdp"),
        P("replica", "fsdp"),
        P("replica", "fsdp", None),
        P("replica", "fsdp", None),
    )
    return jax.shard_map(
        shards,
        mesh=mesh,
        in_specs=placed,
        out_specs=(P("replica", "fsdp"), P("replica", "fsdp"), P("replica", "fsdp", None)),
        check_vma=False,
    )
```

time: 140 us -> 116 us (0.83)
  Pallas kernels: 129 us -> 115 us
  other arithmetic: 6.39 us -> 0 us
  local copies, waits for them, and re-layouts: 3.14 us -> 0 us
    pallas_call x1 -> x2, Pallas kernels: 129 us -> 115 us  [the longest x1 112 us: shards(): pl.pallas_call(kernel, out_shape=(outer, outer, hidden), in_specs=[any_sp...]
    broadcast_in_dim x1 -> x0, other arithmetic: 5.36 us -> none  [shards(): return (new_params, new_momentum, hidden_out[None])]
    unnamed x9 -> x0, local copies, waits for them, and re-layouts: 1.86 us -> none
where the time goes in v2:
time: 116 us
  Pallas kernels  115 us (99%)
    pallas_call x1, Pallas kernels, shards(): pl.pallas_call(kernel, out_shape=(outer, outer, hidden), in_specs=[any_sp...  112 us
    pallas_call x1, Pallas kernels, shards(): pl.pallas_call(store, out_shape=(hidden, outer, outer), in_specs=[any_spa...  2.49 us

profile of v2, /device:TPU:1, one launch (start us, length us, event | category | flops | bytes accessed | tf_op | source)
XLA Modules:
  0.0 115.6 jit_solution(17532287235526945445)
XLA Ops:
  0.6 112.5 %shard_map.85 = (f32[448,448]{1,0:T(8,128)S(1)}, f32[448,448]{1,0:T(8,128)S(1)}, bf16[256,7168]{1,0:T(8,128)(2,1)S(1)}) custom-call(s32[448,3584]{1,0:T(8,128)} %bitcast.7, s32[28,1,448]{2,1,0:T(1,128)} %bitcast.10, f32[448,448]{1,0:T(8,128)} %params.1, f32[448,448]{1,0:T(8,128)} %momentum.1, bf16[256,3584]{1,0:T(8,128)(2,1)} %bitcast.9, ...), custom_call_target="tpu_custom_call" | custom-call | tf_op jit(solution)/shard_map/pallas_call | solution.py:400
  113.1 2.5 %shard_map.86 = (bf16[256,7168]{1,0:T(8,128)(2,1)}, f32[448,448]{1,0:T(8,128)}, f32[448,448]{1,0:T(8,128)}) custom-call(bf16[256,7168]{1,0:T(8,128)(2,1)S(1)} %get-tuple-element.9.hidden, f32[448,448]{1,0:T(8,128)S(1)} %get-tuple-element.10.params, f32[448,448]{1,0:T(8,128)S(1)} %get-tuple-element.11.momentum), custom_call_target="tpu_custom_call" | custom-call | tf_op jit(solution)/shard_map/pallas_call | solution.py:438

commit v3 on v2

--- a/solution.py
+++ b/solution.py
@@ -13,6 +13,8 @@
 TOK = 256
 PAIR = 896
 PIECE = 224
+LATE = 128
+EARLY = PAIR - LATE
 SEND = 7 * PIECE
 VMEM_LIMIT = 48 * 2**20
 
@@ -37,8 +39,8 @@
 def kernel(
     codes, exponents, params, momentum, attention, residual,
     params_out, momentum_out, hidden_out,
-    codes_v, exp_v, deltas, received, par_v, mom_v, summed, block, block_in, weight, att, outs, got, hid,
-    local_sem, rs_s, rs_r, at_s, at_r, sw_s, sw_r, sib_s, sib_r, xs, xr, zs, zr, os_, or_, save_sem,
+    codes_v, exp_v, deltas, received, par_v, mom_v, block, block_in, weight, late, att, outs, got, hid,
+    local_sem, rs_s, rs_r, at_s, at_r, sw_s, sw_r, sib_s, sib_r, late_s, late_r, xs, xr, zs, zr, os_, or_, save_sem, late_save,
 ):
     r = lax.axis_index("replica")
     f = lax.axis_index("fsdp")
@@ -49,28 +51,31 @@
     x2 = lax.rem(x + 2, 4)
     xp = xh * 2 + (1 - xl)
     zu, zd, z2 = lax.rem(z + 1, 4), lax.rem(z + 3, 4), lax.rem(z + 2, 4)
-    yu, yd = lax.rem(y + 1, 4), lax.rem(y + 3, 4)
+    yu, yd, y2 = lax.rem(y + 1, 4), lax.rem(y + 3, 4), lax.rem(y + 2, 4)
     sibling = device(x, y, z, 1 - c)
     to_xp, to_xo = device(xp, y, z, c), device(xo, y, z, c)
     to_zu, to_zd = device(x, y, zu, c), device(x, y, zd, c)
     to_yu, to_yd = device(x, yu, z, c), device(x, yd, z, c)
 
     barrier = pltpu.get_barrier_semaphore()
-    partners = [sibling, to_xp, to_xo, to_yu, to_yd, device(x, lax.rem(y + 2, 4), z, c)]
-    partners += [to_zu, to_zd, device(x, y, z2, c)]
+    partners = [sibling, to_xp, to_xo, to_yu, to_yd, device(x, y2, z, c)]
+    partners += [to_zu, to_zd, device(x, y, z2, c), device(x2, y, z, c)]
     for partner in partners:
         pl.semaphore_signal(barrier, inc=1, device_id=partner, device_id_type=MESH)
 
     z_order = [z2, zu, zd, z]
     exp_copy = pltpu.make_async_copy(exponents, exp_v, local_sem.at[8])
     exp_copy.start()
-    code_copies = []
-    for i, zz in enumerate(z_order):
-        copy = pltpu.make_async_copy(
-            codes.at[:, pl.ds(pl.multiple_of(zz * PAIR, 128), PAIR)], codes_v.at[i], local_sem.at[i]
+    code_copies = [
+        pltpu.make_async_copy(
+            codes.at[pl.ds(h % 2 * PIECE, PIECE), pl.ds(pl.multiple_of(z_order[h // 2] * PAIR, 128), PAIR)],
+            codes_v.at[h % 3],
+            local_sem.at[9 + h],
         )
+        for h in range(8)
+    ]
+    for copy in code_copies[:3]:
         copy.start()
-        code_copies.append(copy)
     par_copy = pltpu.make_async_copy(params, par_v, local_sem.at[4])
     mom_copy = pltpu.make_async_copy(momentum, mom_v, local_sem.at[5])
     att_copy = pltpu.make_async_copy(attention, att.at[y], local_sem.at[6])
@@ -102,22 +107,29 @@
     rs, other = [], 1 - xl
     exp_copy.wait()
     for i, zz in enumerate(z_order):
-        code_copies[i].wait()
         scale = [scale_of(exp_v[7 * zz + t]) for t in range(7)]
         scale = jnp.concatenate(scale + [jnp.zeros((1, COLS), F32)], axis=0)
         scale = jnp.concatenate([scale, jnp.zeros((8, 64), F32)], axis=1).T[:COLS]
 
-        def tile(t):
-            return codes_v[i, :, 128 * t : 128 * (t + 1)].astype(F32) * scale[:, t : t + 1]
-
-        for t in range(3):
-            deltas[2 * zz, t * COLS : (t + 1) * COLS] = tile(t).astype(BF16)
-            deltas[2 * zz + 1, t * COLS : (t + 1) * COLS] = tile(t + 4).astype(BF16)
-        mid = tile(3)
-        turned = pltpu.roll(mid, 64, 1)
-        top, bottom = mid[:PIECE], mid[PIECE:]
-        deltas[2 * zz, 3 * COLS :] = jnp.where(lane, top, turned[PIECE:]).astype(BF16)
-        deltas[2 * zz + 1, 3 * COLS :] = jnp.where(lane, turned[:PIECE], bottom).astype(BF16)
+        middles = []
+        for h in (2 * i, 2 * i + 1):
+            first_col = h % 2 * PIECE
+            code_copies[h].wait()
+
+            def tile(t):
+                code = codes_v[h % 3, :, 128 * t : 128 * (t + 1)].astype(F32)
+                return code * scale[first_col : first_col + PIECE, t : t + 1]
+
+            for t in range(3):
+                rows = slice(t * COLS + first_col, t * COLS + first_col + PIECE)
+                deltas[2 * zz, rows] = tile(t).astype(BF16)
+                deltas[2 * zz + 1, rows] = tile(t + 4).astype(BF16)
+            middles.append(tile(3))
+            if h + 3 < 8:
+                code_copies[h + 3].start()
+        top, bottom = middles
+        deltas[2 * zz, 3 * COLS :] = jnp.where(lane, top, pltpu.roll(bottom, 64, 1)).astype(BF16)
+        deltas[2 * zz + 1, 3 * COLS :] = jnp.where(lane, pltpu.roll(top, 64, 1), bottom).astype(BF16)
         if i == 0:
             pair = send(deltas.at[2 * zz + other], received.at[0], rs_s.at[0], rs_r.at[0], to_xp)
         elif i < 3:
@@ -141,12 +153,6 @@
     add(near, (1, 2))
     rs.append(send(deltas.at[near], received.at[6], rs_s.at[6], rs_r.at[6], to_xp))
 
-    att_copy.wait()
-    at0.wait_recv()
-    at2 = send(att.at[yd, low], att.at[yd, low], at_s.at[2], at_r.at[2], to_yu)
-    at1.wait_recv()
-    at4 = send(att.at[yu, high], att.at[yu, high], at_s.at[4], at_r.at[4], to_yd)
-
     for copy in (rs[1], rs[3], rs[4], rs[5]):
         copy.wait_recv()
 
@@ -156,41 +162,48 @@
             acc = acc + received[k, pl.ds(rows, size)].astype(F32)
         return acc
 
+    par_copy.wait()
+    mom_copy.wait()
+
+    def outer_step(rows, piece, size):
+        outer_grad = piece[:size, :COLS] / 8
+        new_momentum = 0.9 * mom_v[rows] + outer_grad
+        new_params = par_v[rows] - 0.7 * (outer_grad + 0.9 * new_momentum)
+        mom_v[rows] = new_momentum
+        par_v[rows] = new_params
+        block[rows] = jnp.concatenate(
+            [new_params, jnp.zeros((size, 64), F32)], axis=1
+        ).astype(BF16)
+
     fill = jnp.zeros((64, 128), F32)
     for t in range(3):
         piece = jnp.concatenate([total(t * COLS, COLS), fill], axis=0).T
-        summed[pl.ds(pl.multiple_of(xl * 64 + t * 128, 64), 128)] = piece[:, :COLS]
+        outer_step(pl.ds(pl.multiple_of(xl * 64 + t * 128, 64), 128), piece, 128)
     packed = total(3 * COLS, PIECE)
     piece = jnp.concatenate([packed, pltpu.roll(packed, 64, 1), fill], axis=0).T
-    summed[pl.ds(pl.multiple_of((1 - xl) * 384, 64), 64)] = piece[:64, :COLS]
-
-    par_copy.wait()
-    mom_copy.wait()
-    outer_grad = summed[...] / 8
-    new_momentum = 0.9 * mom_v[...] + outer_grad
-    new_params = par_v[...] - 0.7 * (outer_grad + 0.9 * new_momentum)
-    mom_v[...] = new_momentum
-    par_v[...] = new_params
-    block[...] = jnp.concatenate(
-        [new_params, jnp.zeros((COLS, 64), F32)], axis=1
-    ).astype(BF16)
+    outer_step(pl.ds(pl.multiple_of((1 - xl) * 384, 64), 64), piece, 64)
     away = pl.ds(pl.multiple_of((1 - c) * PIECE, 16), PIECE)
-    keep = pl.ds(pl.multiple_of(c * PIECE, 16), PIECE)
     swap = send(block.at[away], block_in, sw_s, sw_r, sibling)
     par_save = pltpu.make_async_copy(par_v, params_out, local_sem.at[4])
     mom_save = pltpu.make_async_copy(mom_v, momentum_out, local_sem.at[5])
     par_save.start()
     mom_save.start()
     swap.wait_recv()
-    mine, theirs = block[keep].astype(F32), block_in[...].astype(F32)
     first = c == 0
-    left = jnp.where(first, mine, theirs)
-    right = pltpu.roll(jnp.where(first, theirs, mine), 64, 1)
-    seam = jnp.where(lane, left[:, 384:], right[:, :128])
+    seam_lane = lax.broadcasted_iota(jnp.int32, (112, 128), 1) < 64
+    lanes = pl.ds(pl.multiple_of(xh * LATE, 128), LATE)
     own_rows = pl.ds(pl.multiple_of(r * COLS + c * PIECE, 16), PIECE)
-    weight[xh, own_rows, :384] = left[:, :384].astype(BF16)
-    weight[xh, own_rows, 384:512] = seam.astype(BF16)
-    weight[xh, own_rows, 512:] = right[:, 128:].astype(BF16)
+    for part in range(2):
+        ours = block[pl.ds(pl.multiple_of(c * PIECE + part * 112, 16), 112)].astype(F32)
+        theirs = block_in[pl.ds(part * 112, 112)].astype(F32)
+        left = jnp.where(first, ours, theirs)
+        right = pltpu.roll(jnp.where(first, theirs, ours), 64, 1)
+        seam = jnp.where(seam_lane, left[:, 384:], right[:, :128])
+        rows = pl.ds(pl.multiple_of(r * COLS + c * PIECE + part * 112, 16), 112)
+        weight[xh, rows, :384] = left[:, :384].astype(BF16)
+        weight[xh, rows, 384:512] = seam.astype(BF16)
+        weight[xh, rows, 512:] = right[:, 128 : EARLY - 384].astype(BF16)
+        late[y, z, xl, 2 * c + part, :, lanes] = right[:, EARLY - 384 :].astype(BF16)
 
     def unit(x_, z_, part, lo=0, size=112):
         start = (2 * z_ + lax.rem(x_, 2)) * COLS + c * PIECE + part * 112 + lo
@@ -214,6 +227,16 @@
         k = n_z[0]
         n_z[0] += 1
         return send(ref, ref, zs.at[k], zr.at[k], to)
+
+    def late_send(k, ref, to):
+        return send(ref, ref, late_s.at[k], late_r.at[k], to)
+
+    to_y2, to_z2, to_x2 = device(x, y2, z, c), device(x, y, z2, c), device(x2, y, z, c)
+    mine = pl.ds(pl.multiple_of(2 * c, 2), 2)
+    late_y = [
+        late_send(k, late.at[y, z, xl, mine, :, lanes], to)
+        for k, to in enumerate((to_yu, to_yd, to_y2))
+    ]
 
     XP, XO, ZU, ZD = to_xp, to_xo, to_zu, to_zd
     own_shares, late_shares = [], []
@@ -233,6 +256,12 @@
     def both(u, d, u_, d_):
         u.append(along_z(u_, ZU))
         d.append(along_z(d_, ZD))
+
+    att_copy.wait()
+    at0.wait_recv()
+    at2 = send(att.at[yd, low], att.at[yd, low], at_s.at[2], at_r.at[2], to_yu)
+    at1.wait_recv()
+    at4 = send(att.at[yu, high], att.at[yu, high], at_s.at[4], at_r.at[4], to_yd)
 
     pz_u.wait_recv()
     pz2_u = along_z(unit(x, zd, 0, 0, 64), ZU)
@@ -289,16 +318,19 @@
     for copy in own_shares:
         copy.wait_recv()
 
-    for copy in (at2, at3, at4, at5):
+    for copy in (at3, at5):
         copy.wait_recv()
 
     def place(side, yy):
         columns = xh if side == 0 else 1 - xh
-        return pl.ds(pl.multiple_of(yy * 1792 + columns * PAIR, 128), PAIR)
+        return pl.ds(pl.multiple_of(yy * 1792 + columns * PAIR, 128), EARLY)
 
     def finish(side, i, value):
-        here = place(side, lax.rem(y + 6 - i * (i + 1) // 2, 4))
-        hid[:, here] = (hid[:, here].astype(F32) + value.astype(F32)).astype(BF16)
+        here = place(side, lax.rem(y + 11 - 2 * i - i // 2, 4))
+        for k in range(0, EARLY, 256):
+            part = pl.ds(pl.multiple_of(here.start + k, 128), 256)
+            total = hid[:, part].astype(F32) + value[:, k : k + 256].astype(F32)
+            hid[:, part] = total.astype(BF16)
         pltpu.make_async_copy(
             hid.at[:, here], hidden_out.at[:, here], save_sem.at[side, i]
         ).start()
@@ -317,7 +349,7 @@
         columns = xh if side == 0 else 1 - xh
 
         def step(i, carry):
-            yy = lax.rem(y + 2 + i * (i + 1) // 2, 4)
+            yy = lax.rem(y + 1 + 2 * i + i // 2, 4)
             result = jnp.dot(att[yy], weight[columns], preferred_element_type=F32).astype(BF16)
 
             @pl.when(i < 3)
@@ -334,6 +366,16 @@
         lax.fori_loop(begin, end, step, 0)
 
     res_copy.wait()
+    for copy in late_y:
+        copy.wait_recv()
+    late_z = [
+        late_send(3 + k, late.at[:, z, xl, 2 * c, :, lanes], to)
+        for k, to in enumerate((to_zu, to_zd, to_z2))
+    ]
+    late_x = [
+        late_send(6 + k, late.at[:, z, xl, 2 * c + 1, :, lanes], to)
+        for k, to in enumerate((to_xp, to_xo, to_x2))
+    ]
     multiply(0, 0, 1)
     qx2_o.wait_recv()
     qx2_p.wait_recv()
@@ -341,10 +383,27 @@
     late_shares.append(share(unit(x2, z, 1)))
     got_z(2, late_shares)
     qz2[2] = along_z(unit(xo, zd, 1), ZU)
-    multiply(0, 1, 3)
+    multiply(0, 1, 2)
     got_z(3, late_shares)
     qz2[3] = along_z(unit(x2, zu, 1), ZD)
-    multiply(0, 3, 4)
+    at2.wait_recv()
+    at4.wait_recv()
+    multiply(0, 2, 4)
+    for copy in late_z:
+        copy.wait_recv()
+    late_zx = [
+        late_send(9 + k, late.at[:, :, xl, 2 * c, :, lanes], to)
+        for k, to in enumerate((to_xp, to_xo))
+    ]
+    late_pairs = [late_send(17, late.at[:, :, xl, 2 * c, :, lanes], sibling)]
+    for copy in late_x:
+        copy.wait_recv()
+    late_xz = [
+        late_send(11 + k, late.at[:, z, :, 2 * c + 1], to)
+        for k, to in enumerate((to_zu, to_zd))
+    ]
+    late_pairs.append(late_send(18, late.at[:, z, :, 2 * c + 1], sibling))
+
     for j in (0, 1, 2, 3):
         px2[j].wait_recv()
         late_shares.append(share(unit(x2, z_units[j], 0)))
@@ -355,14 +414,64 @@
         copy.wait_recv()
     multiply(1, 0, 4)
 
-    for side in range(2):
-
-        def arrive(i, carry):
+    def late_x_unit(x_, lo, size):
+        there = pl.ds(pl.multiple_of(x_ // 2 * LATE, 128), LATE)
+        return late.at[:, lo : lo + size, lax.rem(x_, 2), 2 * c, :, there]
+
+    def late_z_unit(z_, lo, size):
+        return late.at[lo : lo + size, z_, :, 2 * c + 1]
+
+    late_zx[0].wait_recv()
+    fx0 = late_send(13, late_x_unit(xp, 0, 2), to_xo)
+    late_pairs.append(late_send(19, late_x_unit(xp, 0, 4), sibling))
+    late_zx[1].wait_recv()
+    fx1 = late_send(14, late_x_unit(xo, 2, 2), to_xp)
+    late_pairs.append(late_send(20, late_x_unit(xo, 0, 4), sibling))
+    late_xz[0].wait_recv()
+    fz0 = late_send(15, late_z_unit(zd, 0, 2), to_zu)
+    late_pairs.append(late_send(21, late_z_unit(zd, 0, 4), sibling))
+    late_xz[1].wait_recv()
+    fz1 = late_send(16, late_z_unit(zu, 2, 2), to_zd)
+    late_pairs.append(late_send(22, late_z_unit(zu, 0, 4), sibling))
+
+    def arrive(side):
+        def step(i, carry):
             block_copy(side, i, to_yu).wait_recv()
             finish(side, i, got[side, i])
             return carry
 
-        lax.fori_loop(0, 3, arrive, 0)
+        lax.fori_loop(0, 3, step, 0)
+
+    arrive(0)
+    for copy in (fx0, fx1):
+        copy.wait_recv()
+    late_pairs.append(late_send(23, late_x_unit(x2, 0, 4), sibling))
+    for copy in (fz0, fz1):
+        copy.wait_recv()
+    late_pairs.append(late_send(24, late_z_unit(z2, 0, 4), sibling))
+    for copy in late_pairs:
+        copy.wait_recv()
+
+    def late_step(yy, carry):
+        result = jnp.zeros((TOK, 2 * LATE), F32)
+        for k in range(4):
+            result = result + jnp.dot(
+                att[y, :, k * PAIR : (k + 1) * PAIR],
+                late[yy, k].reshape(PAIR, 2 * LATE),
+                preferred_element_type=F32,
+            )
+        result = result.astype(BF16)
+        for k in range(2):
+            here = pl.ds(pl.multiple_of(yy * 1792 + k * PAIR + EARLY, 128), LATE)
+            value = result[:, k * LATE : (k + 1) * LATE].astype(F32)
+            hid[:, here] = (hid[:, here].astype(F32) + value).astype(BF16)
+            pltpu.make_async_copy(
+                hid.at[:, here], hidden_out.at[:, here], late_save.at[yy, k]
+            ).start()
+        return carry
+
+    lax.fori_loop(0, 4, late_step, 0)
+    arrive(1)
 
     for copy in pending:
         copy.wait_send()
@@ -376,6 +485,10 @@
             ).wait()
             if i < 3:
                 block_copy(side, i, to_yu).wait_send()
+            there = pl.ds(i * 1792 + side * PAIR + EARLY, LATE)
+            pltpu.make_async_copy(
+                hid.at[:, there], hidden_out.at[:, there], late_save.at[i, side]
+            ).wait()
 
 
 def store(hidden, params, momentum, hidden_out, params_out, momentum_out, sem):
@@ -403,29 +516,31 @@
         in_specs=[any_space] * 6,
         out_specs=(any_space, any_space, any_space),
         scratch_shapes=[
-            pltpu.VMEM((4, COLS, PAIR), jnp.int32),
+            pltpu.VMEM((3, PIECE, PAIR), jnp.int32),
             pltpu.VMEM((4 * 7, 1, COLS), jnp.int32),
             pltpu.VMEM((8, SEND, 128), BF16),
             pltpu.VMEM((7, SEND, 128), BF16),
             pltpu.VMEM((COLS, COLS), F32),
             pltpu.VMEM((COLS, COLS), F32),
-            pltpu.VMEM((COLS, COLS), F32),
             pltpu.VMEM((COLS, 512), BF16),
             pltpu.VMEM((PIECE, 512), BF16),
-            pltpu.VMEM((2, KDIM, PAIR), BF16),
+            pltpu.VMEM((2, KDIM, EARLY), BF16),
+            pltpu.VMEM((4, 4, 2, 4, 112, 2 * LATE), BF16),
             pltpu.VMEM((4, TOK, KDIM), BF16),
-            pltpu.VMEM((2, 3, TOK, PAIR), BF16),
-            pltpu.VMEM((2, 3, TOK, PAIR), BF16),
+            pltpu.VMEM((2, 3, TOK, EARLY), BF16),
+            pltpu.VMEM((2, 3, TOK, EARLY), BF16),
             pltpu.VMEM((TOK, 4 * 2 * PAIR), BF16),
-            dma((9,)),
+            dma((17,)),
             dma((7,)), dma((7,)),
             dma((6,)), dma((6,)),
             dma, dma,
             dma((31,)), dma((31,)),
+            dma((25,)), dma((25,)),
             dma((16,)), dma((16,)),
             dma((16,)), dma((16,)),
             dma((2, 3)), dma((2, 3)),
             dma((2, 4)),
+            dma((4, 2)),
         ],
         compiler_params=pltpu.CompilerParams(
             collective_id=0, has_side_effects=True, vmem_limit_bytes=VMEM_LIMIT

time: 116 us -> 109 us (0.940)
  Pallas kernels: 115 us -> 109 us
    pallas_call x1, Pallas kernels: 112 us -> 106 us  [shards(): pl.pallas_call(kernel, out_shape=(outer, outer, hidden), in_specs=[any_sp...]
where the time goes in v3:
time: 109 us
  Pallas kernels  109 us (100%)
    pallas_call x1, Pallas kernels, shards(): pl.pallas_call(kernel, out_shape=(outer, outer, hidden), in_specs=[any_sp...  106 us
    pallas_call x1, Pallas kernels, shards(): pl.pallas_call(store, out_shape=(hidden, outer, outer), in_specs=[any_spa...  2.49 us

profile of v3, /device:TPU:1, one launch (start us, length us, event | category | flops | bytes accessed | tf_op | source)
XLA Modules:
  0.0 109.3 jit_solution(4024153387081356749)
XLA Ops:
  0.6 106.1 %shard_map.85 = (f32[448,448]{1,0:T(8,128)S(1)}, f32[448,448]{1,0:T(8,128)S(1)}, bf16[256,7168]{1,0:T(8,128)(2,1)S(1)}) custom-call(s32[448,3584]{1,0:T(8,128)} %bitcast.7, s32[28,1,448]{2,1,0:T(1,128)} %bitcast.10, f32[448,448]{1,0:T(8,128)} %params.1, f32[448,448]{1,0:T(8,128)} %momentum.1, bf16[256,3584]{1,0:T(8,128)(2,1)} %bitcast.9, ...), custom_call_target="tpu_custom_call" | custom-call | tf_op jit(solution)/shard_map/pallas_call | solution.py:513
  106.8 2.5 %shard_map.86 = (bf16[256,7168]{1,0:T(8,128)(2,1)}, f32[448,448]{1,0:T(8,128)}, f32[448,448]{1,0:T(8,128)}) custom-call(bf16[256,7168]{1,0:T(8,128)(2,1)S(1)} %get-tuple-element.9.hidden, f32[448,448]{1,0:T(8,128)S(1)} %get-tuple-element.10.params, f32[448,448]{1,0:T(8,128)S(1)} %get-tuple-element.11.momentum), custom_call_target="tpu_custom_call" | custom-call | tf_op jit(solution)/shard_map/pallas_call | solution.py:553

commit v4 on v3

--- a/solution.py
+++ b/solution.py
@@ -434,21 +434,22 @@
     fz1 = late_send(16, late_z_unit(zu, 2, 2), to_zd)
     late_pairs.append(late_send(22, late_z_unit(zu, 0, 4), sibling))
 
-    def arrive(side):
+    def arrive(side, begin, end):
         def step(i, carry):
             block_copy(side, i, to_yu).wait_recv()
             finish(side, i, got[side, i])
             return carry
 
-        lax.fori_loop(0, 3, step, 0)
-
-    arrive(0)
+        lax.fori_loop(begin, end, step, 0)
+
+    arrive(0, 0, 3)
     for copy in (fx0, fx1):
         copy.wait_recv()
     late_pairs.append(late_send(23, late_x_unit(x2, 0, 4), sibling))
     for copy in (fz0, fz1):
         copy.wait_recv()
     late_pairs.append(late_send(24, late_z_unit(z2, 0, 4), sibling))
+    arrive(1, 0, 2)
     for copy in late_pairs:
         copy.wait_recv()
 
@@ -471,7 +472,7 @@
         return carry
 
     lax.fori_loop(0, 4, late_step, 0)
-    arrive(1)
+    arrive(1, 2, 3)
 
     for copy in pending:
         copy.wait_send()

time: 109 us -> 109 us (level)
  no operation moved by 1% of the time
where the time goes in v4:
time: 109 us
  Pallas kernels  109 us (100%)
    pallas_call x1, Pallas kernels, shards(): pl.pallas_call(kernel, out_shape=(outer, outer, hidden), in_specs=[any_sp...  106 us
    pallas_call x1, Pallas kernels, shards(): pl.pallas_call(store, out_shape=(hidden, outer, outer), in_specs=[any_spa...  2.49 us

profile of v4, /device:TPU:1, one launch (start us, length us, event | category | flops | bytes accessed | tf_op | source)
XLA Modules:
  0.0 109.3 jit_solution(13227836769996326682)
XLA Ops:
  0.6 106.1 %shard_map.85 = (f32[448,448]{1,0:T(8,128)S(1)}, f32[448,448]{1,0:T(8,128)S(1)}, bf16[256,7168]{1,0:T(8,128)(2,1)S(1)}) custom-call(s32[448,3584]{1,0:T(8,128)} %bitcast.7, s32[28,1,448]{2,1,0:T(1,128)} %bitcast.10, f32[448,448]{1,0:T(8,128)} %params.1, f32[448,448]{1,0:T(8,128)} %momentum.1, bf16[256,3584]{1,0:T(8,128)(2,1)} %bitcast.9, ...), custom_call_target="tpu_custom_call" | custom-call | tf_op jit(solution)/shard_map/pallas_call | solution.py:514
  106.8 2.5 %shard_map.86 = (bf16[256,7168]{1,0:T(8,128)(2,1)}, f32[448,448]{1,0:T(8,128)}, f32[448,448]{1,0:T(8,128)}) custom-call(bf16[256,7168]{1,0:T(8,128)(2,1)S(1)} %get-tuple-element.9.hidden, f32[448,448]{1,0:T(8,128)S(1)} %get-tuple-element.10.params, f32[448,448]{1,0:T(8,128)S(1)} %get-tuple-element.11.momentum), custom_call_target="tpu_custom_call" | custom-call | tf_op jit(solution)/shard_map/pallas_call | solution.py:554
